TPU v7x, 256 devices: a whole 4x4x8 slice. The times are simulated.
256 devices in a mesh: row: 4 (over x), col: 4 (over y), depth: 16 (over z, core).
Axes of the slice: x: 4, y: 4, z: 8, core: 2. Of those that a mesh axis runs over, the one named last changes fastest.
Arguments:
- activations: bfloat16 [8192, 14848], P(('row', 'depth'), 'col'), may hold values from -0.1875 to 0.1875
- pre_act: bfloat16 [8192, 8192], P(('col', 'depth'), 'row'), may hold values from -8 to 8
- grad_act: bfloat16 [8192, 8192], P(('col', 'depth'), 'row'), may hold values from -6 to 6
- quant_weight: bfloat16 [14848, 8192], P('col', 'row'), may hold values from -0.046875 to 0.046875
- block_scale: float32 [116, 8192], P('col', 'row'), may hold values from 0.5 to 2
Outputs:
- grad_input: bfloat16 [8192, 14848], P(('row', 'depth'), 'col')
- grad_weight: bfloat16 [14848, 8192], P(('col', 'depth'), 'row')
All inputs are finite; a program needn't handle non-finite values.
Results may differ from a plain program's by a relative error of at most 0.0058.
Values may be sent and summed in bfloat16 or wider, within the bound.
A program may use at most 192 MiB of HBM per device.

v0:
```python
import jax
import jax.numpy as jnp
from jax import lax
from jax.sharding import PartitionSpec as P

BLOCK = 128


inv_sqrt_two = 0.7071067811865476
inv_sqrt_tau = 0.3989422804014327


def gelu_slope(values):
    return (
        0.5 * (1.0 + lax.erf(values * inv_sqrt_two))
        + values * jnp.exp(-0.5 * values * values) * inv_sqrt_tau
    )


def local(activations, pre_act, grad_act, quant_weight, block_scale):
    width_local = quant_weight.shape[0]
    hidden_local = quant_weight.shape[1]
    scaled = (
        quant_weight.astype(jnp.float32).reshape(block_scale.shape[0], BLOCK, hidden_local)
        * block_scale[:, None, :]
    )
    weight = scaled.reshape(width_local, hidden_local).astype(jnp.bfloat16)
    grad_pre = (grad_act.astype(jnp.float32) * gelu_slope(pre_act.astype(jnp.float32))).astype(
        jnp.bfloat16
    )
    layer_grad = lax.all_gather(grad_pre, "col", axis=0, tiled=True)
    layer_acts = lax.all_gather(activations, "row", axis=0, tiled=True)
    grad_weight = lax.psum_scatter(
        lax.dot_general(
            layer_acts, layer_grad, (((0,), (0,)), ((), ())), preferred_element_type=jnp.float32
        ),
        "depth",
        scatter_dimension=0,
        tiled=True,
    ).astype(jnp.bfloat16)
    grad_input = lax.psum_scatter(
        lax.dot_general(
            layer_grad, weight, (((1,), (1,)), ((), ())), preferred_element_type=jnp.float32
        ),
        "row",
        scatter_dimension=0,
        tiled=True,
    ).astype(jnp.bfloat16)
    return (grad_input, grad_weight)


def solution(mesh):
    placed = (
        P(("row", "depth"), "col"),
        P(("col", "depth"), "row"),
        P(("col", "depth"), "row"),
        P("col", "row"),
        P("col", "row"),
    )
    return jax.shard_map(
        local,
        mesh=mesh,
        in_specs=placed,
        out_specs=(P(("row", "depth"), "col"), P(("col", "depth"), "row")),
        check_vma=False,
    )
```

profile of v0, /device:TPU:1, one launch (start us, length us, event | category | flops | bytes accessed | tf_op | source)
XLA Modules:
  0.0 357.2 jit_solution(6595278770743294782)
XLA Ops:
  7.2 0.0 all-gather.3.cloned.1.call-start
  7.2 2.5 fusion.8
  9.7 0.0 all-gather.3.cloned.1.call-update
  9.7 0.0 all-gather.5.cloned.1.call-start
  9.8 0.7 all-gather.5.cloned.1.call-update
  10.5 0.0 reduce-scatter.5.cloned.1.call-start
  10.5 11.7 %fusion = bf16[3712,2048]{1,0:T(8,128)(2,1)} fusion(bf16[3712,2048]{1,0:T(8,128)(2,1)} %param.8, f32[29,2048]{1,0:T(8,128)} %param.9), kind=kLoop, calls=%fused_computation.1 | loop fusion | flops 22806528 | bytes 30646272 | tf_op jit(solution)/shard_map/convert_element_type | solution.py:27
  22.3 25.4 %all-gather.3.cloned.1.call-done = bf16[512,2048]{1,0:T(8,128)(2,1)} async-done(((bf16[128,2048]{1,0:T(8,128)(2,1)}), bf16[512,2048]{1,0:T(8,128)(2,1)}) %all-gather.3.cloned.1.call-update) | async-done | bytes 2097168 | tf_op jit(solution)/shard_map/all_gather | solution.py:31
  47.6 14.8 %fusion.9 = f32[512,3712]{1,0:T(8,128)} fusion(bf16[512,2048]{1,0:T(8,128)(2,1)} %all-gather.3.cloned.1.call-done, bf16[3712,2048]{1,0:T(8,128)(2,1)} %fusion), kind=kOutput, calls=%fused_computation.15 | convolution fusion | flops 7784628224 | bytes 24903680 | tf_op jit(solution)/shard_map/dot_general | solution.py:42
  62.4 0.0 copy-start
  62.4 0.0 reduce-scatter.5.cloned.1.call-update
  62.4 0.0 reduce-scatter.7.cloned.1.call-start
  62.5 34.6 %all-gather.5.cloned.1.call-done = bf16[512,3712]{1,0:T(8,128)(2,1)} async-done(((bf16[128,3712]{1,0:T(8,128)(2,1)}), bf16[512,3712]{1,0:T(8,128)(2,1)}) %all-gather.5.cloned.1.call-update) | async-done | bytes 3801104 | tf_op jit(solution)/shard_map/all_gather | solution.py:32
  97.0 0.0 copy-done
  97.0 17.4 %convolution_bitcast_fusion = f32[3712,2048]{0,1:T(8,128)} fusion(bf16[512,2048]{1,0:T(8,128)(2,1)S(1)} %copy-done, bf16[512,3712]{1,0:T(8,128)(2,1)} %all-gather.5.cloned.1.call-done), kind=kOutput, calls=%fused_computation.2 | convolution fusion | flops 7784628224 | bytes 36306944 | tf_op jit(solution)/shard_map/dot_general | solution.py:34
  114.4 30.4 %copy.9 = f32[3712,2048]{1,0:T(8,128)} copy(f32[3712,2048]{0,1:T(8,128)} %convolution_bitcast_fusion) | data formatting | bytes 60817408
  144.9 0.0 reduce-scatter.7.cloned.1.call-update
  144.9 32.3 %reduce-scatter.5.cloned.1.call-done = f32[128,3712]{1,0:T(8,128)} async-done(((f32[512,3712]{1,0:T(8,128)}), f32[128,3712]{1,0:T(8,128)}) %reduce-scatter.5.cloned.1.call-update) | async-done | bytes 1900560 | tf_op jit(solution)/shard_map/reduce_scatter | solution.py:41
  177.2 2.6 convert_element_type.26
  179.8 168.0 %reduce-scatter.7.cloned.1.call-done = f32[232,2048]{1,0:T(8,128)} async-done(((f32[3712,2048]{1,0:T(8,128)}), f32[232,2048]{1,0:T(8,128)}) %reduce-scatter.7.cloned.1.call-update) | async-done | bytes 1900560
  347.7 1.7 copy.10
  349.4 1.3 copy.8
Async XLA Ops:
  7.2 40.5 %all-gather.3.cloned.1.call-start = ((), (), s32[]{:S(2)}) async-start(), calls=%async_computation.2 | async-start | bytes 2621440 | tf_op jit(solution)/shard_map/all_gather | solution.py:31
  9.7 87.3 %all-gather.5.cloned.1.call-start = ((), (), s32[]{:S(2)}) async-start(), calls=%async_computation.4 | async-start | bytes 4751360 | tf_op jit(solution)/shard_map/all_gather | solution.py:32
  10.5 166.7 %reduce-scatter.5.cloned.1.call-start = ((), (), s32[]{:S(2)}) async-start(), calls=%async_computation.3 | async-start | bytes 9502720 | tf_op jit(solution)/shard_map/reduce_scatter | solution.py:41
  62.4 34.6 %copy-start = (bf16[512,2048]{1,0:T(8,128)(2,1)S(1)}, bf16[512,2048]{1,0:T(8,128)(2,1)}, u32[]{:S(2)}) copy-start(bf16[512,2048]{1,0:T(8,128)(2,1)} %all-gather.3.cloned.1.call-done) | copy-start | bytes 6291460
  62.4 285.3 %reduce-scatter.7.cloned.1.call-start = ((), (), s32[]{:S(2)}) async-start(), calls=%async_computation.5 | async-start | bytes 32309248
Sparse Core Ops, SparseCore 0:
  10.4 37.2 all-gather.2
  49.4 47.5 all-gather.4
  99.6 77.5 reduce-scatter.4
  179.6 168.0 reduce-scatter.6
where the time goes:
time: 358 us; the launch traced here: 357 us
  waiting for transfers between devices  261 us (73%)
  local copies, waits for them, and re-layouts  33.4 us (9%)
  matrix products  32.1 us (9%)
  other arithmetic  16.8 us (5%)
  between operations  13.8 us (4%)
    unnamed x5, waiting for transfers between devices  169 us
    all_gather x1, waiting for transfers between devices, local(): layer_acts = lax.all_gather(activations, 'row', axis=0, tiled=True)  34.6 us
    unnamed x5, local copies, waits for them, and re-layouts  33.4 us
    reduce_scatter x1, waiting for transfers between devices, local(): lax.psum_scatter(lax.dot_general(layer_grad, weight, (((1,), (1,)), ((),...  32.3 us
    all_gather x1, waiting for transfers between devices, local(): layer_grad = lax.all_gather(grad_pre, 'col', axis=0, tiled=True)  25.4 us
    dot_general x1, matrix products, local(): lax.dot_general(layer_acts, layer_grad, (((0,), (0,)), ((), ())), preferr...  17.4 us
    dot_general x1, matrix products, local(): lax.dot_general(layer_grad, weight, (((1,), (1,)), ((), ())), preferred_e...  14.8 us
    convert_element_type x1, other arithmetic, local(): weight = scaled.reshape(width_local, hidden_local).astype(jnp.bfloat16)  11.7 us
  transfers between devices with their start and end apart: 4, of which 4 were waited for; matrix products, arithmetic and copies ran while one was open for 22% of the time, Pallas kernels for 0%

commit v1 on v0

v1 whole, which is shorter than its diff:
```python
import jax
import jax.numpy as jnp
from jax import lax
from jax.experimental import pallas as pl
from jax.experimental.pallas import tpu as pltpu
from jax.sharding import PartitionSpec as P

MESH = pl.DeviceIdType.MESH
BF16, F32 = jnp.bfloat16, jnp.float32
NX, NY, NZ = 4, 4, 8
TOK = 128
FL = 2048
DL = 3712
CH = 232
FQ = 512
PAIR = 256
NP = 7
BASE = 1920
MID = 1792

inv_sqrt_two = 0.7071067811865476
inv_sqrt_tau = 0.3989422804014327


def gelu_slope(values):
    return (
        0.5 * (1.0 + lax.erf(values * inv_sqrt_two))
        + values * jnp.exp(-0.5 * values * values) * inv_sqrt_tau
    )


def kernel(
    acts_h, pre_h, grad_h, qw_h, scale_h, gi_h, gw_h,
    acts, pre, grad, scale, wq, wm, at32, asend, at, gb, zs, zr,
    gis, gism, gir, girm, gsx, go, gwo,
    in_sem, w_sem, a_send, a_recv, g_send, g_recv, f_send, f_recv,
    z_send, z_recv, i_send, i_recv, s_send, s_recv, out_sem,
):
    x, y, depth = lax.axis_index("row"), lax.axis_index("col"), lax.axis_index("depth")
    z, c = depth // 2, lax.rem(depth, 2)
    oc = 1 - c

    def dev(dx, dy, dz, core):
        return (
            lax.rem(x + dx, NX),
            lax.rem(y + dy, NY),
            lax.rem(z + dz, NZ) * 2 + core,
        )

    def remote(src, dst, send, recv, where):
        pltpu.make_async_remote_copy(
            src_ref=src, dst_ref=dst, send_sem=send, recv_sem=recv,
            device_id=where, device_id_type=MESH,
        ).start()

    def wait(ref, sem):
        pltpu.make_async_copy(ref, ref, sem).wait()

    loads = [
        pltpu.make_async_copy(pre_h, pre, in_sem.at[0]),
        pltpu.make_async_copy(grad_h, grad, in_sem.at[1]),
        pltpu.make_async_copy(acts_h, acts, in_sem.at[2]),
        pltpu.make_async_copy(scale_h, scale, in_sem.at[3]),
    ]
    for cp in loads:
        cp.start()
    w_loads = [
        pltpu.make_async_copy(
            qw_h.at[pl.ds(pl.multiple_of(c * BASE + PAIR * i, 128), PAIR)], wq.at[i], w_sem.at[i]
        )
        for i in range(NP)
    ] + [pltpu.make_async_copy(qw_h.at[pl.ds(MID, 128)], wm, w_sem.at[NP])]
    for cp in w_loads:
        cp.start()

    partners = (
        [dev(dx, 0, 0, k) for dx in range(1, NX) for k in (c, oc)]
        + [dev(0, dy, 0, c) for dy in range(1, NY)]
        + [dev(0, 0, 1, c), dev(0, 0, NZ - 1, c), dev(0, 0, 0, oc)]
    )
    barrier = pltpu.get_barrier_semaphore()
    for who in partners:
        pl.semaphore_signal(barrier, inc=1, device_id=who, device_id_type=MESH)

    own_row = pl.multiple_of((c * NY + y) * TOK, TOK)

    def slope(q):
        def rows(r, carry):
            at_r = pl.ds(pl.multiple_of(r * 16, 16), 16)
            cols = pl.ds(q * FQ, FQ)
            g = grad[at_r, cols].astype(F32) * gelu_slope(pre[at_r, cols].astype(F32))
            gb[pl.ds(pl.multiple_of(own_row + r * 16, 16), 16), cols] = g.astype(BF16)
            return carry

        lax.fori_loop(0, TOK // 16, rows, 0)

    def send_slope(q):
        block = gb.at[pl.ds(own_row, TOK), pl.ds(q * FQ, FQ)]
        for dy in (1, 3, 2):
            remote(block, block, g_send.at[q], g_recv.at[q], dev(0, dy, 0, c))

    def forward_slope(q):
        wait(gb.at[pl.ds(0, 3 * TOK), pl.ds(q * FQ, FQ)], g_recv.at[q])
        layer = gb.at[pl.ds(pl.multiple_of(c * NY * TOK, TOK), NY * TOK), pl.ds(q * FQ, FQ)]
        remote(layer, layer, f_send.at[q], f_recv.at[q], dev(0, 0, 0, oc))

    def wait_slope(q):
        wait(gb.at[pl.ds(0, NY * TOK), pl.ds(q * FQ, FQ)], f_recv.at[q])

    lanes = pl.ds(pl.multiple_of((c * NX + x) * TOK, TOK), TOK)

    def send_acts(d):
        for par in (0, 1):
            core = c if par == 0 else oc
            p = 2 * lax.rem(z + d, NZ) + core
            block = at32[pl.ds(pl.multiple_of(p * CH, 8), CH), :].astype(BF16)
            slot = 2 * d + par
            asend[slot] = block
            if par == 0:
                at[d, :, lanes] = block
            for dx in (1, 3, 2):
                remote(
                    asend.at[slot], at.at[d, :, lanes], a_send.at[d], a_recv.at[d], dev(dx, 0, 0, core)
                )
            if par == 1:
                remote(asend.at[slot], at.at[d, :, lanes], a_send.at[d], a_recv.at[d], dev(0, 0, 0, oc))

    def wait_acts(d):
        wait(at.at[d, :, pl.ds(0, 7 * TOK)], a_recv.at[d])

    def part(d, q):
        return lax.dot_general(
            at[d % NZ], gb[:, pl.ds(q * FQ, FQ)], (((1,), (0,)), ((), ())),
            preferred_element_type=F32,
        )

    def slot_of(r, q):
        return r * 4 + q if r < 3 else 12 + q % 2

    def ring(way, r, q):
        long = (q < 2) == (way == 0)
        offset = (4 if long else 3) - r
        if offset == 0:
            return
        d = offset if way == 0 else -offset
        mine = part(d, q)
        s = slot_of(r, q)
        if r == 0:
            src = zs.at[way, q]
        else:
            came = slot_of(r - 1, q)
            src = zr.at[way, came]
            wait(src, z_recv.at[way, came])
            mine = mine + src[...].astype(F32)
        src[...] = mine.astype(BF16)
        remote(
            src, zr.at[way, s], z_send.at[way, s], z_recv.at[way, s],
            dev(0, 0, 1 if way == 0 else NZ - 1, c),
        )

    def last(q):
        total = part(0, q)
        for way in (0, 1):
            long = (q < 2) == (way == 0)
            s = slot_of(3 if long else 2, q)
            wait(zr.at[way, s], z_recv.at[way, s])
            total = total + zr[way, s].astype(F32)
        gwo[:, pl.ds(q * FQ, FQ)] = total.astype(BF16)

    nt = (((1,), (1,)), ((), ()))

    def rescale(ref, row):
        by = scale[pl.ds(row, 1), :]

        def rows(r, carry):
            at_r = pl.ds(pl.multiple_of(r * 16, 16), 16)
            ref[at_r, :] = (ref[at_r, :].astype(F32) * by).astype(BF16)
            return carry

        lax.fori_loop(0, 8, rows, 0)

    def inputs(i):
        w_loads[i].wait()
        if i < NP:
            for h in (0, 1):
                rescale(wq.at[i, pl.ds(128 * h, 128)], c * 15 + 2 * i + h)
            for k in (0, 1):
                got = lax.dot_general(
                    gb[pl.ds(k * NX * TOK, NX * TOK), :], wq[i], nt, preferred_element_type=F32
                )
                gis[i, k] = got.reshape(NX, TOK, PAIR).astype(BF16)
            for dx in (1, 3, 2):
                to = lax.rem(x + dx, NX)
                remote(
                    gis.at[i, :, to], gir.at[i, dx - 1], i_send.at[i], i_recv.at[i], dev(dx, 0, 0, c)
                )
        else:
            rescale(wm, 14)
            got = lax.dot_general(
                gb[pl.ds(pl.multiple_of(c * NX * TOK, TOK), NX * TOK), :], wm[...], nt,
                preferred_element_type=F32,
            )
            gism[...] = got.reshape(NX, TOK, 128).astype(BF16)
            for dx in (1, 3, 2):
                to = lax.rem(x + dx, NX)
                remote(gism.at[to], girm.at[dx - 1], i_send.at[i], i_recv.at[i], dev(dx, 0, 0, c))

    def inputs_done(i):
        if i < NP:
            wait(gir.at[i], i_recv.at[i])
            cols = pl.ds(pl.multiple_of(c * BASE + PAIR * i, 128), PAIR)

            def total(k):
                got = gis[i, pl.ds(k, 1), pl.ds(x, 1)].reshape(TOK, PAIR).astype(F32)
                for s in range(3):
                    got = got + gir[i, s, pl.ds(k, 1)].reshape(TOK, PAIR).astype(F32)
                return got.astype(BF16)

            gsx[i] = total(oc)
            remote(gsx.at[i], go.at[:, cols], s_send, s_recv, dev(0, 0, 0, oc))
            go[:, cols] = total(c)
        else:
            wait(girm, i_recv.at[i])
            got = gism[pl.ds(x, 1)].reshape(TOK, 128).astype(F32)
            for s in range(3):
                got = got + girm[s].astype(F32)
            go[:, pl.ds(MID, 128)] = got.astype(BF16)

    loads[0].wait()
    loads[1].wait()
    slope(0)
    pl.semaphore_wait(barrier, len(partners))
    send_slope(0)
    loads[2].wait()

    def turn(b, carry):
        at_b = pl.ds(pl.multiple_of(b * 128, 128), 128)
        at32[at_b, :] = acts[:, at_b].astype(F32).T
        return carry

    lax.fori_loop(0, DL // 128, turn, 0)
    send_acts(4)
    slope(1)
    send_slope(1)
    send_acts(5)
    send_acts(3)
    for q in (2, 3):
        slope(q)
        send_slope(q)
    for d in (2, 6, 1, 7, 0):
        send_acts(d)

    forward_slope(0)
    loads[3].wait()
    for q in range(4):
        wait_slope(q)
        if q == 0:
            wait_acts(4)
        if q == 2:
            wait_acts(3)
        if q < 2:
            ring(0, 0, q)
            if q == 0:
                wait_acts(5)
            ring(1, 0, q)
        else:
            ring(1, 0, q)
            ring(0, 0, q)
        if q < 3:
            forward_slope(q + 1)
    inputs(0)
    inputs(1)
    wait_acts(2)
    wait_acts(6)
    for q in range(4):
        for way in (0, 1):
            ring(way, 1, q)
        inputs(2 + q)
    wait_acts(1)
    wait_acts(7)
    for q in range(4):
        for way in (0, 1):
            ring(way, 2, q)
        if q < 2:
            inputs(6 + q)
    for i in (0, 1, 2):
        inputs_done(i)
    wait_acts(0)
    for q in (0, 1):
        ring(0, 3, q)
        ring(1, 3, q + 2)
    for i in (3, 4, 5, 6, 7):
        inputs_done(i)
    wait(go.at[:, pl.ds(0, MID)], s_recv)
    out_i = pltpu.make_async_copy(go, gi_h, out_sem.at[0])
    out_i.start()
    for q in range(4):
        last(q)
    out_w = pltpu.make_async_copy(gwo, gw_h, out_sem.at[1])
    out_w.start()

    for q in range(4):
        wait(gb.at[pl.ds(0, 3 * TOK), pl.ds(q * FQ, FQ)], g_send.at[q])
        wait(gb.at[pl.ds(0, NY * TOK), pl.ds(q * FQ, FQ)], f_send.at[q])
    for d in range(NZ):
        wait(at.at[d, :, pl.ds(0, 7 * TOK)], a_send.at[d])
    for way in (0, 1):
        for s in range(14):
            wait(zr.at[way, s], z_send.at[way, s])
    for i in range(NP):
        wait(gir.at[i], i_send.at[i])
    wait(girm, i_send.at[NP])
    wait(go.at[:, pl.ds(0, MID)], s_send)
    out_i.wait()
    out_w.wait()


def local(activations, pre_act, grad_act, quant_weight, block_scale):
    dma = pltpu.SemaphoreType.DMA
    hbm = pl.BlockSpec(memory_space=pl.ANY)
    return pl.pallas_call(
        kernel,
        out_shape=(
            jax.ShapeDtypeStruct((TOK, DL), BF16),
            jax.ShapeDtypeStruct((CH, FL), BF16),
        ),
        in_specs=[hbm] * 5,
        out_specs=(hbm, hbm),
        scratch_shapes=[
            pltpu.VMEM((TOK, DL), BF16),
            pltpu.VMEM((TOK, FL), BF16),
            pltpu.VMEM((TOK, FL), BF16),
            pltpu.VMEM((29, FL), F32),
            pltpu.VMEM((NP, PAIR, FL), BF16),
            pltpu.VMEM((128, FL), BF16),
            pltpu.VMEM((DL, TOK), F32),
            pltpu.VMEM((2 * NZ, CH, TOK), BF16),
            pltpu.VMEM((NZ, CH, 8 * TOK), BF16),
            pltpu.VMEM((8 * TOK, FL), BF16),
            pltpu.VMEM((2, 4, CH, FQ), BF16),
            pltpu.VMEM((2, 14, CH, FQ), BF16),
            pltpu.VMEM((NP, 2, NX, TOK, PAIR), BF16),
            pltpu.VMEM((NX, TOK, 128), BF16),
            pltpu.VMEM((NP, 3, 2, TOK, PAIR), BF16),
            pltpu.VMEM((3, TOK, 128), BF16),
            pltpu.VMEM((NP, TOK, PAIR), BF16),
            pltpu.VMEM((TOK, DL), BF16),
            pltpu.VMEM((CH, FL), BF16),
            dma((4,)), dma((NP + 1,)),
            dma((NZ,)), dma((NZ,)),
            dma((4,)), dma((4,)), dma((4,)), dma((4,)),
            dma((2, 14)), dma((2, 14)),
            dma((NP + 1,)), dma((NP + 1,)),
            dma, dma, dma((2,)),
        ],
        compiler_params=pltpu.CompilerParams(
            collective_id=0, has_side_effects=True, vmem_limit_bytes=56 * 2**20
        ),
        cost_estimate=pl.CostEstimate(
            flops=2 * 2 * 512 * FL * DL, bytes_accessed=20 * 2**20, transcendentals=2 * TOK * FL
        ),
    )(activations, pre_act, grad_act, quant_weight, block_scale)


def solution(mesh):
    placed = (
        P(("row", "depth"), "col"),
        P(("col", "depth"), "row"),
        P(("col", "depth"), "row"),
        P("col", "row"),
        P("col", "row"),
    )
    return jax.shard_map(
        local,
        mesh=mesh,
        in_specs=placed,
        out_specs=(P(("row", "depth"), "col"), P(("col", "depth"), "row")),
        check_vma=False,
    )
```

time: 358 us -> 105 us (0.29)
  waiting for transfers between devices: 261 us -> 0 us
  Pallas kernels: 0 us -> 100 us
  matrix products: 32.1 us -> 0 us
  local copies, waits for them, and re-layouts: 33.4 us -> 4.41 us
  other arithmetic: 16.8 us -> 0 us
  between operations: 13.8 us -> 0.64 us
    unnamed x5 -> x0, waiting for transfers between devices: 169 us -> none
    pallas_call x0 -> x1, Pallas kernels: none -> 100 us  [local(): pl.pallas_call(kernel, out_shape=(jax.ShapeDtypeStruct((TOK, DL), BF16),...]
    all_gather x2 -> x0, waiting for transfers between devices: 59.9 us -> none  [the longest x1 34.6 us: local(): layer_acts = lax.all_gather(activations, 'row', axis=0, tiled=True)]
    reduce_scatter x1 -> x0, waiting for transfers between devices: 32.3 us -> none  [local(): lax.psum_scatter(lax.dot_general(layer_grad, weight, (((1,), (1,)), ((),...]
    dot_general x2 -> x0, matrix products: 32.1 us -> none  [the longest x1 17.4 us: local(): lax.dot_general(layer_acts, layer_grad, (((0,), (0,)), ((), ())), preferr...]
    unnamed x5 -> x2, local copies, waits for them, and re-layouts: 33.4 us -> 4.41 us
    convert_element_type x3 -> x0, other arithmetic: 16.8 us -> none  [the longest x1 11.7 us: local(): weight = scaled.reshape(width_local, hidden_local).astype(jnp.bfloat16)]
  transfers between devices with their start and end apart: 4 -> 0, of which waited for: 4 -> 0; matrix products, arithmetic and copies ran while one was open for 22% -> 0% of each run, Pallas kernels for 0% -> 0%
where the time goes in v1:
time: 105 us
  Pallas kernels  100 us (95%)
  local copies, waits for them, and re-layouts  4.41 us (4%)
    pallas_call x1, Pallas kernels, local(): pl.pallas_call(kernel, out_shape=(jax.ShapeDtypeStruct((TOK, DL), BF16),...  100 us
    unnamed x2, local copies, waits for them, and re-layouts  4.41 us

profile of v1, /device:TPU:1, one launch (start us, length us, event | category | flops | bytes accessed | tf_op | source)
XLA Modules:
  0.0 105.0 jit_solution(14987443517372385893)
XLA Ops:
  0.6 100.0 %shard_map.68 = (bf16[128,3712]{1,0:T(8,128)(2,1)}, bf16[232,2048]{1,0:T(8,128)(2,1)}) custom-call(bf16[128,3712]{1,0:T(8,128)(2,1)} %acts_h.1, bf16[128,2048]{1,0:T(8,128)(2,1)} %pre_h.1, bf16[128,2048]{1,0:T(8,128)(2,1)} %grad_h.1, bf16[3712,2048]{1,0:T(8,128)(2,1)} %qw_h.1, f32[29,2048]{1,0:T(8,128)} %scale_h.1), custom_call_target="tpu_custom_call" | custom-call | flops 15569256448 | bytes 20971520 | tf_op jit(solution)/shard_map/pallas_call | solution.py:321
  100.6 2.2 %copy.9 = bf16[128,3712]{1,0:T(8,128)(2,1)} copy(bf16[128,3712]{1,0:T(8,128)(2,1)} %get-tuple-element.4) | data formatting | bytes 1900544
  102.8 2.2 %copy.10 = bf16[232,2048]{1,0:T(8,128)(2,1)} copy(bf16[232,2048]{1,0:T(8,128)(2,1)} %get-tuple-element.5) | data formatting | bytes 1900544

commit v2 on v1

v2 whole, which is shorter than its diff:
```python
import jax
import jax.numpy as jnp
from jax import lax
from jax.experimental import pallas as pl
from jax.experimental.pallas import tpu as pltpu
from jax.sharding import PartitionSpec as P

MESH = pl.DeviceIdType.MESH
BF16, F32 = jnp.bfloat16, jnp.float32
NX, NY, NZ = 4, 4, 8
TOK = 128
FL = 2048
DL = 3712
CH = 232
FQ = 512
SLICES = ((0, 256), (256, 256), (512, 256), (768, 256), (1024, 512), (1536, 512))
NS = len(SLICES)
DIRECT = (4, 5, 3)
WIN = 640
PAIR = 256
NP = 7
BASE = 1920
MID = 1792

inv_sqrt_two = 0.7071067811865476
inv_sqrt_tau = 0.3989422804014327


def gelu_slope(values):
    return (
        0.5 * (1.0 + lax.erf(values * inv_sqrt_two))
        + values * jnp.exp(-0.5 * values * values) * inv_sqrt_tau
    )


def kernel(
    acts_h, pre_h, grad_h, qw_h, scale_h, gi_h, gw_h,
    acts, pre, grad, scale, wq, wm, at32, asend, at, gb, zs, zr,
    gis, gism, gir, girm, gia, giam, gsx, go, gwo, own,
    in_sem, w_sem, a_send, a_recv, h_send, h_recv, g_send, g_recv, f_send, f_recv,
    z_send, z_recv, i_send, i_recv, j_send, j_recv, s_send, s_recv, out_sem,
):
    x, y, depth = lax.axis_index("row"), lax.axis_index("col"), lax.axis_index("depth")
    z, c = depth // 2, lax.rem(depth, 2)
    oc = 1 - c

    def dev(dx, dy, dz, core):
        return (
            lax.rem(x + dx, NX),
            lax.rem(y + dy, NY),
            lax.rem(z + dz, NZ) * 2 + core,
        )

    def remote(src, dst, send, recv, where):
        pltpu.make_async_remote_copy(
            src_ref=src, dst_ref=dst, send_sem=send, recv_sem=recv,
            device_id=where, device_id_type=MESH,
        ).start()

    def wait(ref, sem):
        pltpu.make_async_copy(ref, ref, sem).wait()

    head, tail = pl.ds(*SLICES[0]), pl.ds(SLICES[1][0], FL - SLICES[1][0])
    loads = [
        pltpu.make_async_copy(pre_h.at[:, head], pre.at[:, head], in_sem.at[0]),
        pltpu.make_async_copy(grad_h.at[:, head], grad.at[:, head], in_sem.at[1]),
        pltpu.make_async_copy(acts_h, acts, in_sem.at[2]),
        pltpu.make_async_copy(pre_h.at[:, tail], pre.at[:, tail], in_sem.at[3]),
        pltpu.make_async_copy(grad_h.at[:, tail], grad.at[:, tail], in_sem.at[4]),
        pltpu.make_async_copy(scale_h, scale, in_sem.at[5]),
    ]
    for cp in loads[:5]:
        cp.start()
    w_loads = [
        pltpu.make_async_copy(
            qw_h.at[pl.ds(pl.multiple_of(c * BASE + PAIR * i, 128), PAIR)], wq.at[i], w_sem.at[i]
        )
        for i in range(NP)
    ] + [pltpu.make_async_copy(qw_h.at[pl.ds(MID, 128)], wm, w_sem.at[NP])]

    partners = (
        [dev(dx, 0, 0, k) for dx in range(1, NX) for k in (c, oc)]
        + [dev(0, dy, 0, c) for dy in range(1, NY)]
        + [dev(0, 0, 1, c), dev(0, 0, NZ - 1, c), dev(0, 0, 0, oc)]
    )
    barrier = pltpu.get_barrier_semaphore()
    for who in partners:
        pl.semaphore_signal(barrier, inc=1, device_id=who, device_id_type=MESH)

    own_row = pl.multiple_of((c * NY + y) * TOK, TOK)

    def hidden(q):
        return pl.ds(*SLICES[q])

    def slope(q):
        def rows(r, carry):
            at_r = pl.ds(pl.multiple_of(r * 16, 16), 16)
            cols = hidden(q)
            g = grad[at_r, cols].astype(F32) * gelu_slope(pre[at_r, cols].astype(F32))
            gb[pl.ds(pl.multiple_of(own_row + r * 16, 16), 16), cols] = g.astype(BF16)
            return carry

        lax.fori_loop(0, TOK // 16, rows, 0)

    def send_slope(q):
        block = gb.at[pl.ds(own_row, TOK), hidden(q)]
        for dy in (1, 3, 2):
            remote(block, block, g_send.at[q], g_recv.at[q], dev(0, dy, 0, c))

    def forward_slope(q):
        wait(gb.at[pl.ds(0, 3 * TOK), hidden(q)], g_recv.at[q])
        layer = gb.at[pl.ds(pl.multiple_of(c * NY * TOK, TOK), NY * TOK), hidden(q)]
        remote(layer, layer, f_send.at[q], f_recv.at[q], dev(0, 0, 0, oc))

    def wait_slope(q):
        wait(gb.at[pl.ds(0, NY * TOK), hidden(q)], f_recv.at[q])

    lanes = pl.ds(pl.multiple_of((c * NX + x) * TOK, TOK), TOK)

    def turn_acts(d):
        owner = lax.rem(z + d, NZ)
        tile = jnp.minimum(owner * (2 * CH) // 128, (DL - WIN) // 128)
        for i in range(WIN // 128):
            cols = pl.ds(pl.multiple_of((tile + i) * 128, 128), 128)
            at32[pl.ds(128 * i, 128), :] = acts[:, cols].astype(F32).T
        skip = owner * (2 * CH) - tile * 128
        for par in (0, 1):
            core = c if par == 0 else oc
            block = at32[pl.ds(pl.multiple_of(skip + core * CH, 8), CH), :].astype(BF16)
            asend[2 * d + par] = block
            if par == 0:
                at[d, :, lanes] = block

    def post_acts(d):
        for par in (0, 1):
            core = c if par == 0 else oc
            block = asend.at[2 * d + par]
            for dx in (1, 3, 2) if d in DIRECT else (1, 3):
                remote(block, at.at[d, :, lanes], a_send.at[d], a_recv.at[d], dev(dx, 0, 0, core))
            if par == 1:
                remote(block, at.at[d, :, lanes], a_send.at[d], a_recv.at[d], dev(0, 0, 0, oc))

    def send_acts(d):
        turn_acts(d)
        post_acts(d)

    def hand_on(d):
        wait(at.at[d, :, pl.ds(0, 5 * TOK)], a_recv.at[d])
        for dx, core in ((1, c), (3, oc)):
            block = at.at[
                d, :, pl.ds(pl.multiple_of((core * NX + lax.rem(x - dx + NX, NX)) * TOK, TOK), TOK)
            ]
            remote(block, block, h_send.at[d], h_recv.at[d], dev(dx, 0, 0, c))

    def wait_acts(d):
        if d in DIRECT:
            wait(at.at[d, :, pl.ds(0, 7 * TOK)], a_recv.at[d])
        else:
            wait(at.at[d, :, pl.ds(0, 2 * TOK)], h_recv.at[d])

    def part(d, q):
        return lax.dot_general(
            at[d % NZ], gb[:, hidden(q)], (((1,), (0,)), ((), ())),
            preferred_element_type=F32,
        )

    def is_long(way, q):
        return q % 2 == way

    def landing(way, r, q):
        return zr.at[way, r, :, hidden(q)]

    def ring(way, r, q):
        offset = (4 if is_long(way, q) else 3) - r
        if offset == 0:
            return
        mine = part(offset if way == 0 else -offset, q)
        if r == 0:
            src = zs.at[way, :, hidden(q)]
        else:
            src = landing(way, r - 1, q)
            wait(src, z_recv.at[way, r - 1, q])
            mine = mine + src[...].astype(F32)
        src[...] = mine.astype(BF16)
        remote(
            src, landing(way, r, q), z_send.at[way, r, q], z_recv.at[way, r, q],
            dev(0, 0, 1 if way == 0 else NZ - 1, c),
        )

    def add_short(q):
        way = 1 if is_long(0, q) else 0
        total = part(0, q)
        wait(landing(way, 2, q), z_recv.at[way, 2, q])
        own[:, hidden(q)] = total + landing(way, 2, q)[...].astype(F32)

    def add_long(q):
        way = 0 if is_long(0, q) else 1
        wait(landing(way, 3, q), z_recv.at[way, 3, q])
        gwo[:, hidden(q)] = (own[:, hidden(q)] + landing(way, 3, q)[...].astype(F32)).astype(BF16)
        pltpu.make_async_copy(
            gwo.at[:, hidden(q)], gw_h.at[:, hidden(q)], out_sem.at[1 + q]
        ).start()

    nt = (((1,), (1,)), ((), ()))

    def rescale(ref, row):
        by = scale[pl.ds(row, 1), :]

        def rows(r, carry):
            at_r = pl.ds(pl.multiple_of(r * 16, 16), 16)
            ref[at_r, :] = (ref[at_r, :].astype(F32) * by).astype(BF16)
            return carry

        lax.fori_loop(0, 8, rows, 0)

    def inputs(i):
        w_loads[i].wait()
        if i < NP:
            for h in (0, 1):
                rescale(wq.at[i, pl.ds(128 * h, 128)], c * 15 + 2 * i + h)
            for k in (0, 1):
                got = lax.dot_general(
                    gb[pl.ds(k * NX * TOK, NX * TOK), :], wq[i], nt, preferred_element_type=F32
                )
                gis[i, k] = got.reshape(NX, TOK, PAIR).astype(BF16)
            far = lax.rem(x + 2, NX)
            for k, dx in ((0, 1), (1, 3)):
                remote(
                    gis.at[i, k, far], gia.at[i, k], j_send.at[i], j_recv.at[i], dev(dx, 0, 0, c)
                )
        else:
            rescale(wm, 14)
            got = lax.dot_general(
                gb[pl.ds(pl.multiple_of(c * NX * TOK, TOK), NX * TOK), :], wm[...], nt,
                preferred_element_type=F32,
            )
            gism[...] = got.reshape(NX, TOK, 128).astype(BF16)
            far = lax.rem(x + 2, NX)
            for k, dx in ((0, 1), (1, 3)):
                remote(
                    gism.at[far, pl.ds(64 * k, 64)], giam.at[k], j_send.at[i], j_recv.at[i],
                    dev(dx, 0, 0, c),
                )

    def inputs_on(i):
        wait(gia.at[i] if i < NP else giam, j_recv.at[i])
        for k, dx in ((0, 1), (1, 3)):
            to = lax.rem(x + dx, NX)
            if i < NP:
                mine, came = gis.at[i, k, to], gia.at[i, k]
            else:
                mine, came = gism.at[to, pl.ds(64 * k, 64)], giam.at[k]
            mine[...] = (mine[...].astype(F32) + came[...].astype(F32)).astype(BF16)
            if i < NP:
                remote(gis.at[i, :, to], gir.at[i, k], i_send.at[i], i_recv.at[i], dev(dx, 0, 0, c))
            else:
                remote(gism.at[to], girm.at[k], i_send.at[i], i_recv.at[i], dev(dx, 0, 0, c))

    def inputs_done(i):
        if i < NP:
            wait(gir.at[i], i_recv.at[i])
            cols = pl.ds(pl.multiple_of(c * BASE + PAIR * i, 128), PAIR)

            def total(k):
                got = gis[i, pl.ds(k, 1), pl.ds(x, 1)].reshape(TOK, PAIR).astype(F32)
                for s in range(2):
                    got = got + gir[i, s, pl.ds(k, 1)].reshape(TOK, PAIR).astype(F32)
                return got.astype(BF16)

            gsx[i] = total(oc)
            remote(gsx.at[i], go.at[:, cols], s_send, s_recv, dev(0, 0, 0, oc))
            go[:, cols] = total(c)
        else:
            wait(girm, i_recv.at[i])
            got = gism[pl.ds(x, 1)].reshape(TOK, 128).astype(F32)
            for s in range(2):
                got = got + girm[s].astype(F32)
            go[:, pl.ds(MID, 128)] = got.astype(BF16)

    handed, here = set(), set()

    def step(way, r, q):
        offset = (4 if is_long(way, q) else 3) - r
        d = (offset if way == 0 else -offset) % NZ
        if d not in here:
            if d not in DIRECT and d not in handed:
                hand_on(d)
                handed.add(d)
            wait_acts(d)
            here.add(d)
        ring(way, r, q)

    def first_half(q):
        forward_slope(q)
        if q + 2 < NS:
            send_slope(q + 2)

    def pass_on(d):
        hand_on(d)
        handed.add(d)

    loads[2].wait()
    turn_acts(4)
    loads[0].wait()
    loads[1].wait()
    slope(0)
    pl.semaphore_wait(barrier, len(partners))
    send_slope(0)
    post_acts(4)
    loads[3].wait()
    loads[4].wait()
    slope(1)
    send_slope(1)
    for cp in [loads[5]] + w_loads:
        cp.start()
    slope(2)
    slope(3)

    plan = (
        ("F0 A5 W0 000", "S4 F1 A3 W1", "101 S5 F2 W2", "002 100 F3 A6", "W3 103 001 102")
        + ("010 111", "F4 A2 W4 004", "003 104", "F5 A7 W5 105", "005 H6")
        + ("I0 A1 012 113", "H2 I1 110 011", "A0 I2 014 115", "J0 H7 I3", "112 013 J1 I4")
        + ("020 121 H1", "J2 I5 114 015", "H0 J3 I6", "022 123 J4", "I7 120 021 024", "J5 125")
        + ("J6 D0 030 131", "J7 D1 122 023", "D2 032 133", "D3 124 025", "D4 034 135", "D5")
    )
    does = dict(
        F=first_half, A=send_acts, W=wait_slope, H=pass_on, S=slope,
        I=inputs, J=inputs_on, D=inputs_done,
    )
    for word in " ".join(plan).split():
        if word == "I0":
            loads[5].wait()
        if word[0] in does:
            does[word[0]](int(word[1:]))
        else:
            step(*map(int, word))
    if 0 not in here:
        wait_acts(0)
    for q in range(NS):
        add_short(q)
    inputs_done(6)
    inputs_done(7)
    wait(go.at[:, pl.ds(0, MID)], s_recv)
    out_i = pltpu.make_async_copy(go, gi_h, out_sem.at[0])
    out_i.start()
    for q in range(NS):
        add_long(q)

    for q in range(NS):
        wait(gb.at[pl.ds(0, 3 * TOK), hidden(q)], g_send.at[q])
        wait(gb.at[pl.ds(0, NY * TOK), hidden(q)], f_send.at[q])
    for d in range(NZ):
        wait(at.at[d, :, pl.ds(0, (7 if d in DIRECT else 5) * TOK)], a_send.at[d])
        if d not in DIRECT:
            wait(at.at[d, :, pl.ds(0, 2 * TOK)], h_send.at[d])
    for way in (0, 1):
        for q in range(NS):
            for r in range(4 if is_long(way, q) else 3):
                wait(landing(way, r, q), z_send.at[way, r, q])
    for i in range(NP):
        wait(gia.at[i], j_send.at[i])
        wait(gir.at[i], i_send.at[i])
    wait(giam, j_send.at[NP])
    wait(girm, i_send.at[NP])
    wait(go.at[:, pl.ds(0, MID)], s_send)
    out_i.wait()
    for q in range(NS):
        wait(gwo.at[:, hidden(q)], out_sem.at[1 + q])


def copy_out(gi_in, gw_in, gi_out, gw_out, gi, gw, sem):
    pieces = [(pl.ds(32 * i, 32), slice(None)) for i in range(4)]
    bands = [(slice(None), pl.ds(FQ * i, FQ)) for i in range(4)]
    steps = [(gi_in.at[k], gi.at[k], gi_out.at[k]) for k in pieces] + [
        (gw_in.at[k], gw.at[k], gw_out.at[k]) for k in bands
    ]
    into = [pltpu.make_async_copy(src, mid, sem.at[0, i]) for i, (src, mid, _) in enumerate(steps)]
    out = [pltpu.make_async_copy(mid, dst, sem.at[1, i]) for i, (_, mid, dst) in enumerate(steps)]
    for cp in into:
        cp.start()
    for one, two in zip(into, out):
        one.wait()
        two.start()
    for cp in out:
        cp.wait()


def local(activations, pre_act, grad_act, quant_weight, block_scale):
    dma = pltpu.SemaphoreType.DMA
    hbm = pl.BlockSpec(memory_space=pl.ANY)
    shapes = (
        jax.ShapeDtypeStruct((TOK, DL), BF16),
        jax.ShapeDtypeStruct((CH, FL), BF16),
    )
    outs = pl.pallas_call(
        kernel,
        out_shape=shapes,
        in_specs=[hbm] * 5,
        out_specs=(hbm, hbm),
        scratch_shapes=[
            pltpu.VMEM((TOK, DL), BF16),
            pltpu.VMEM((TOK, FL), BF16),
            pltpu.VMEM((TOK, FL), BF16),
            pltpu.VMEM((29, FL), F32),
            pltpu.VMEM((NP, PAIR, FL), BF16),
            pltpu.VMEM((128, FL), BF16),
            pltpu.VMEM((WIN, TOK), F32),
            pltpu.VMEM((2 * NZ, CH, TOK), BF16),
            pltpu.VMEM((NZ, CH, 8 * TOK), BF16),
            pltpu.VMEM((8 * TOK, FL), BF16),
            pltpu.VMEM((2, CH, FL), BF16),
            pltpu.VMEM((2, 4, CH, FL), BF16),
            pltpu.VMEM((NP, 2, NX, TOK, PAIR), BF16),
            pltpu.VMEM((NX, TOK, 128), BF16),
            pltpu.VMEM((NP, 2, 2, TOK, PAIR), BF16),
            pltpu.VMEM((2, TOK, 128), BF16),
            pltpu.VMEM((NP, 2, TOK, PAIR), BF16),
            pltpu.VMEM((2, 64, 128), BF16),
            pltpu.VMEM((NP, TOK, PAIR), BF16),
            pltpu.VMEM((TOK, DL), BF16),
            pltpu.VMEM((CH, FL), BF16),
            pltpu.VMEM((CH, FL), F32),
            dma((6,)), dma((NP + 1,)),
            dma((NZ,)), dma((NZ,)), dma((NZ,)), dma((NZ,)),
            dma((NS,)), dma((NS,)), dma((NS,)), dma((NS,)),
            dma((2, 4, NS)), dma((2, 4, NS)),
            dma((NP + 1,)), dma((NP + 1,)), dma((NP + 1,)), dma((NP + 1,)),
            dma, dma,
            dma((1 + NS,)),
        ],
        compiler_params=pltpu.CompilerParams(
            collective_id=0, has_side_effects=True, vmem_limit_bytes=56 * 2**20
        ),
        cost_estimate=pl.CostEstimate(
            flops=2 * 2 * 512 * FL * DL, bytes_accessed=20 * 2**20, transcendentals=2 * TOK * FL
        ),
    )(activations, pre_act, grad_act, quant_weight, block_scale)
    return pl.pallas_call(
        copy_out,
        out_shape=shapes,
        in_specs=[hbm] * 2,
        out_specs=(hbm, hbm),
        scratch_shapes=[pltpu.VMEM((TOK, DL), BF16), pltpu.VMEM((CH, FL), BF16), dma((2, 8))],
    )(*outs)


def solution(mesh):
    placed = (
        P(("row", "depth"), "col"),
        P(("col", "depth"), "row"),
        P(("col", "depth"), "row"),
        P("col", "row"),
        P("col", "row"),
    )
    return jax.shard_map(
        local,
        mesh=mesh,
        in_specs=placed,
        out_specs=(P(("row", "depth"), "col"), P(("col", "depth"), "row")),
        check_vma=False,
    )
```

time: 105 us -> 102 us (0.971)
  local copies, waits for them, and re-layouts: 4.41 us -> 0 us
    unnamed x2 -> x0, local copies, waits for them, and re-layouts: 4.41 us -> none
    pallas_call x1 -> x2, Pallas kernels: 100 us -> 101 us  [the longest x1 98.2 us: local(): pl.pallas_call(kernel, out_shape=shapes, in_specs=[hbm] * 5, out_specs=(h...]
where the time goes in v2:
time: 102 us; the launch traced here: 101 us
  Pallas kernels  101 us (99%)
    pallas_call x1, Pallas kernels, local(): pl.pallas_call(kernel, out_shape=shapes, in_specs=[hbm] * 5, out_specs=(h...  98.2 us
    pallas_call x1, Pallas kernels, local(): pl.pallas_call(copy_out, out_shape=shapes, in_specs=[hbm] * 2, out_specs=...  2.44 us

profile of v2, /device:TPU:1, one launch (start us, length us, event | category | flops | bytes accessed | tf_op | source)
XLA Modules:
  0.0 101.4 jit_solution(12794728195375749233)
XLA Ops:
  0.6 98.2 %shard_map.68 = (bf16[128,3712]{1,0:T(8,128)(2,1)}, bf16[232,2048]{1,0:T(8,128)(2,1)}) custom-call(bf16[128,3712]{1,0:T(8,128)(2,1)} %acts_h.1, bf16[128,2048]{1,0:T(8,128)(2,1)} %pre_h.1, bf16[128,2048]{1,0:T(8,128)(2,1)} %grad_h.1, bf16[3712,2048]{1,0:T(8,128)(2,1)} %qw_h.1, f32[29,2048]{1,0:T(8,128)} %scale_h.1), custom_call_target="tpu_custom_call" | custom-call | flops 15569256448 | bytes 20971520 | tf_op jit(solution)/shard_map/pallas_call | solution.py:395
  98.8 2.4 %shard_map.69 = (bf16[128,3712]{1,0:T(8,128)(2,1)}, bf16[232,2048]{1,0:T(8,128)(2,1)}) custom-call(bf16[128,3712]{1,0:T(8,128)(2,1)} %get-tuple-element.4.gi_in, bf16[232,2048]{1,0:T(8,128)(2,1)} %get-tuple-element.5.gw_in), custom_call_target="tpu_custom_call" | custom-call | tf_op jit(solution)/shard_map/pallas_call | solution.py:438

commit v3 on v2

--- a/solution.py
+++ b/solution.py
@@ -15,7 +15,7 @@
 FQ = 512
 SLICES = ((0, 256), (256, 256), (512, 256), (768, 256), (1024, 512), (1536, 512))
 NS = len(SLICES)
-DIRECT = (4, 5, 3)
+DIRECT = ()
 WIN = 640
 PAIR = 256
 NP = 7
@@ -38,7 +38,8 @@
     acts, pre, grad, scale, wq, wm, at32, asend, at, gb, zs, zr,
     gis, gism, gir, girm, gia, giam, gsx, go, gwo, own,
     in_sem, w_sem, a_send, a_recv, h_send, h_recv, g_send, g_recv, f_send, f_recv,
-    z_send, z_recv, i_send, i_recv, j_send, j_recv, s_send, s_recv, out_sem,
+    z_send, z_recv, i_send, i_recv, j_send, j_recv, s_send, s_recv,
+    n_send, n_recv, m_send, m_recv, out_sem,
 ):
     x, y, depth = lax.axis_index("row"), lax.axis_index("col"), lax.axis_index("depth")
     z, c = depth // 2, lax.rem(depth, 2)
@@ -90,7 +91,18 @@
     own_row = pl.multiple_of((c * NY + y) * TOK, TOK)
 
     def hidden(q):
-        return pl.ds(*SLICES[q])
+        first, units = SLICES[q % NS]
+        return pl.ds(first + q // NS * FL, units)
+
+    def ship_slope(q):
+        own = pl.ds(own_row, TOK)
+        remote(
+            gb.at[own, hidden(q)], gb.at[own, hidden(NS + q)], n_send.at[q], n_recv.at[q],
+            dev(0, 0, NZ - 1 if q % 2 else 1, c),
+        )
+
+    def take_slope(q):
+        wait(gb.at[pl.ds(0, TOK), hidden(q)], n_recv.at[q - NS])
 
     def slope(q):
         def rows(r, carry):
@@ -144,6 +156,20 @@
         turn_acts(d)
         post_acts(d)
 
+    def ship_acts():
+        for way in (0, 1):
+            for par in (0, 1):
+                remote(
+                    asend.at[8 + par], asend.at[2 * (NZ + way) + par], m_send.at[way, par],
+                    m_recv.at[way, par], dev(0, 0, 1 if way == 0 else NZ - 1, c),
+                )
+
+    def take_acts(d):
+        for par in (0, 1):
+            wait(asend.at[2 * d + par], m_recv.at[d - NZ, par])
+        at[d, :, lanes] = asend[2 * d]
+        post_acts(d)
+
     def hand_on(d):
         wait(at.at[d, :, pl.ds(0, 5 * TOK)], a_recv.at[d])
         for dx, core in ((1, c), (3, oc)):
@@ -160,7 +186,7 @@
 
     def part(d, q):
         return lax.dot_general(
-            at[d % NZ], gb[:, hidden(q)], (((1,), (0,)), ((), ())),
+            at[d], gb[:, hidden(q)], (((1,), (0,)), ((), ())),
             preferred_element_type=F32,
         )
 
@@ -171,12 +197,13 @@
         return zr.at[way, r, :, hidden(q)]
 
     def ring(way, r, q):
-        offset = (4 if is_long(way, q) else 3) - r
-        if offset == 0:
-            return
-        mine = part(offset if way == 0 else -offset, q)
-        if r == 0:
+        long = is_long(way, q)
+        offset = (4 if long else 3) - r
+        mine = part(offset if way == 0 else NZ - offset, q)
+        if r == 0 or (long and r == 1):
             src = zs.at[way, :, hidden(q)]
+            if long:
+                mine = mine + part(NZ + way, NS + q)
         else:
             src = landing(way, r - 1, q)
             wait(src, z_recv.at[way, r - 1, q])
@@ -220,7 +247,7 @@
                 rescale(wq.at[i, pl.ds(128 * h, 128)], c * 15 + 2 * i + h)
             for k in (0, 1):
                 got = lax.dot_general(
-                    gb[pl.ds(k * NX * TOK, NX * TOK), :], wq[i], nt, preferred_element_type=F32
+                    gb[pl.ds(k * NX * TOK, NX * TOK), pl.ds(0, FL)], wq[i], nt, preferred_element_type=F32
                 )
                 gis[i, k] = got.reshape(NX, TOK, PAIR).astype(BF16)
             far = lax.rem(x + 2, NX)
@@ -231,7 +258,7 @@
         else:
             rescale(wm, 14)
             got = lax.dot_general(
-                gb[pl.ds(pl.multiple_of(c * NX * TOK, TOK), NX * TOK), :], wm[...], nt,
+                gb[pl.ds(pl.multiple_of(c * NX * TOK, TOK), NX * TOK), pl.ds(0, FL)], wm[...], nt,
                 preferred_element_type=F32,
             )
             gism[...] = got.reshape(NX, TOK, 128).astype(BF16)
@@ -277,27 +304,34 @@
                 got = got + girm[s].astype(F32)
             go[:, pl.ds(MID, 128)] = got.astype(BF16)
 
-    handed, here = set(), set()
+    handed, here, summed, scaled = set(), set(), set(), False
+
+    def get(d):
+        if d not in here:
+            if d not in DIRECT:
+                pass_on(d)
+            wait_acts(d)
+            here.add(d)
 
     def step(way, r, q):
         offset = (4 if is_long(way, q) else 3) - r
-        d = (offset if way == 0 else -offset) % NZ
-        if d not in here:
-            if d not in DIRECT and d not in handed:
-                hand_on(d)
-                handed.add(d)
-            wait_acts(d)
-            here.add(d)
+        get(offset if way == 0 else NZ - offset)
+        if r == 1 and is_long(way, q):
+            get(NZ + way)
         ring(way, r, q)
 
-    def first_half(q):
-        forward_slope(q)
-        if q + 2 < NS:
-            send_slope(q + 2)
-
     def pass_on(d):
-        hand_on(d)
-        handed.add(d)
+        if d not in handed:
+            hand_on(d)
+            handed.add(d)
+
+    def spread(q):
+        take_slope(q)
+        send_slope(q)
+
+    def own_slice(q):
+        slope(q)
+        ship_slope(q)
 
     loads[2].wait()
     turn_acts(4)
@@ -306,30 +340,35 @@
     slope(0)
     pl.semaphore_wait(barrier, len(partners))
     send_slope(0)
-    post_acts(4)
+    ship_acts()
+    ship_slope(0)
+    send_acts(5)
     loads[3].wait()
     loads[4].wait()
-    slope(1)
+    own_slice(1)
     send_slope(1)
+    send_acts(3)
     for cp in [loads[5]] + w_loads:
         cp.start()
-    slope(2)
-    slope(3)
 
     plan = (
-        ("F0 A5 W0 000", "S4 F1 A3 W1", "101 S5 F2 W2", "002 100 F3 A6", "W3 103 001 102")
-        + ("010 111", "F4 A2 W4 004", "003 104", "F5 A7 W5 105", "005 H6")
-        + ("I0 A1 012 113", "H2 I1 110 011", "A0 I2 014 115", "J0 H7 I3", "112 013 J1 I4")
-        + ("020 121 H1", "J2 I5 114 015", "H0 J3 I6", "022 123 J4", "I7 120 021 024", "J5 125")
-        + ("J6 D0 030 131", "J7 D1 122 023", "D2 032 133", "D3 124 025", "D4 034 135", "D5")
+        ("S3 S2 G2 G3", "F0 S4 H5 G4", "W0 A6 F1 H3", "S5 G5 100 F2", "A2 U6 H6 W2",)
+        + ("U7 102 F3 W1", "001 U8 A7 W3", "003 H2 U9 U10", "U11 110 A1 F4", "112 H7 T8 013",)
+        + ("011 W4 104 T9", "H1 F5 A0 122", "120 W5 005 I4", "F7 H9 F6 114", "023 021 H8 W6",)
+        + ("F8 I0 H0 015", "F9 J4 W8 I2", "012 010 W9 113", "J0 124 F10 I5", "D4 J2 W10 014",)
+        + ("025 D0 F11 123", "022 J5 I1 020", "D2 W11 115 133", "D5 I3 024 J1", "I6 J3 W7 111",)
+        + ("125 I7 D1 J6", "032 121 D3 J7", "030 D6 D7 135", "034 131",)
     )
     does = dict(
-        F=first_half, A=send_acts, W=wait_slope, H=pass_on, S=slope,
-        I=inputs, J=inputs_on, D=inputs_done,
+        F=forward_slope, A=send_acts, W=wait_slope, H=pass_on, S=own_slice,
+        G=send_slope, T=take_acts, U=spread, I=inputs, J=inputs_on, D=inputs_done,
     )
     for word in " ".join(plan).split():
-        if word == "I0":
+        if word[0] == "I" and not scaled:
             loads[5].wait()
+            scaled = True
+        if word[0] == "D":
+            summed.add(int(word[1:]))
         if word[0] in does:
             does[word[0]](int(word[1:]))
         else:
@@ -338,8 +377,9 @@
         wait_acts(0)
     for q in range(NS):
         add_short(q)
-    inputs_done(6)
-    inputs_done(7)
+    for i in range(NP + 1):
+        if i not in summed:
+            inputs_done(i)
     wait(go.at[:, pl.ds(0, MID)], s_recv)
     out_i = pltpu.make_async_copy(go, gi_h, out_sem.at[0])
     out_i.start()
@@ -349,13 +389,20 @@
     for q in range(NS):
         wait(gb.at[pl.ds(0, 3 * TOK), hidden(q)], g_send.at[q])
         wait(gb.at[pl.ds(0, NY * TOK), hidden(q)], f_send.at[q])
-    for d in range(NZ):
+    for q in range(NS, 2 * NS):
+        wait(gb.at[pl.ds(0, 3 * TOK), hidden(q)], g_send.at[q])
+        wait(gb.at[pl.ds(0, NY * TOK), hidden(q)], f_send.at[q])
+        wait(gb.at[pl.ds(0, TOK), hidden(q)], n_send.at[q - NS])
+    for way in (0, 1):
+        for par in (0, 1):
+            wait(asend.at[8 + par], m_send.at[way, par])
+    for d in (0, 1, 2, 3, 5, 6, 7, 8, 9):
         wait(at.at[d, :, pl.ds(0, (7 if d in DIRECT else 5) * TOK)], a_send.at[d])
         if d not in DIRECT:
             wait(at.at[d, :, pl.ds(0, 2 * TOK)], h_send.at[d])
     for way in (0, 1):
         for q in range(NS):
-            for r in range(4 if is_long(way, q) else 3):
+            for r in range(1, 4) if is_long(way, q) else range(3):
                 wait(landing(way, r, q), z_send.at[way, r, q])
     for i in range(NP):
         wait(gia.at[i], j_send.at[i])
@@ -405,9 +452,9 @@
             pltpu.VMEM((NP, PAIR, FL), BF16),
             pltpu.VMEM((128, FL), BF16),
             pltpu.VMEM((WIN, TOK), F32),
-            pltpu.VMEM((2 * NZ, CH, TOK), BF16),
-            pltpu.VMEM((NZ, CH, 8 * TOK), BF16),
-            pltpu.VMEM((8 * TOK, FL), BF16),
+            pltpu.VMEM((2 * NZ + 4, CH, TOK), BF16),
+            pltpu.VMEM((NZ + 2, CH, 8 * TOK), BF16),
+            pltpu.VMEM((8 * TOK, 2 * FL), BF16),
             pltpu.VMEM((2, CH, FL), BF16),
             pltpu.VMEM((2, 4, CH, FL), BF16),
             pltpu.VMEM((NP, 2, NX, TOK, PAIR), BF16),
@@ -421,15 +468,15 @@
             pltpu.VMEM((CH, FL), BF16),
             pltpu.VMEM((CH, FL), F32),
             dma((6,)), dma((NP + 1,)),
-            dma((NZ,)), dma((NZ,)), dma((NZ,)), dma((NZ,)),
-            dma((NS,)), dma((NS,)), dma((NS,)), dma((NS,)),
+            dma((NZ + 2,)), dma((NZ + 2,)), dma((NZ + 2,)), dma((NZ + 2,)),
+            dma((2 * NS,)), dma((2 * NS,)), dma((2 * NS,)), dma((2 * NS,)),
             dma((2, 4, NS)), dma((2, 4, NS)),
             dma((NP + 1,)), dma((NP + 1,)), dma((NP + 1,)), dma((NP + 1,)),
             dma, dma,
-            dma((1 + NS,)),
+            dma((NS,)), dma((NS,)), dma((2, 2)), dma((2, 2)), dma((1 + NS,)),
         ],
         compiler_params=pltpu.CompilerParams(
-            collective_id=0, has_side_effects=True, vmem_limit_bytes=56 * 2**20
+            collective_id=0, has_side_effects=True, vmem_limit_bytes=60 * 2**20
         ),
         cost_estimate=pl.CostEstimate(
             flops=2 * 2 * 512 * FL * DL, bytes_accessed=20 * 2**20, transcendentals=2 * TOK * FL

time: 102 us -> 97.3 us (0.954)
  Pallas kernels: 101 us -> 96.3 us
    pallas_call x1, Pallas kernels: 98.2 us -> 93.9 us  [local(): pl.pallas_call(kernel, out_shape=shapes, in_specs=[hbm] * 5, out_specs=(h...]
where the time goes in v3:
time: 97.3 us; the launch traced here: 97.1 us
  Pallas kernels  96.3 us (99%)
    pallas_call x1, Pallas kernels, local(): pl.pallas_call(kernel, out_shape=shapes, in_specs=[hbm] * 5, out_specs=(h...  93.9 us
    pallas_call x1, Pallas kernels, local(): pl.pallas_call(copy_out, out_shape=shapes, in_specs=[hbm] * 2, out_specs=...  2.44 us

profile of v3, /device:TPU:1, one launch (start us, length us, event | category | flops | bytes accessed | tf_op | source)
XLA Modules:
  0.0 97.1 jit_solution(10820931505249629272)
XLA Ops:
  0.6 93.9 %shard_map.68 = (bf16[128,3712]{1,0:T(8,128)(2,1)}, bf16[232,2048]{1,0:T(8,128)(2,1)}) custom-call(bf16[128,3712]{1,0:T(8,128)(2,1)} %acts_h.1, bf16[128,2048]{1,0:T(8,128)(2,1)} %pre_h.1, bf16[128,2048]{1,0:T(8,128)(2,1)} %grad_h.1, bf16[3712,2048]{1,0:T(8,128)(2,1)} %qw_h.1, f32[29,2048]{1,0:T(8,128)} %scale_h.1), custom_call_target="tpu_custom_call" | custom-call | flops 15569256448 | bytes 20971520 | tf_op jit(solution)/shard_map/pallas_call | solution.py:442
  94.5 2.4 %shard_map.69 = (bf16[128,3712]{1,0:T(8,128)(2,1)}, bf16[232,2048]{1,0:T(8,128)(2,1)}) custom-call(bf16[128,3712]{1,0:T(8,128)(2,1)} %get-tuple-element.4.gi_in, bf16[232,2048]{1,0:T(8,128)(2,1)} %get-tuple-element.5.gw_in), custom_call_target="tpu_custom_call" | custom-call | tf_op jit(solution)/shard_map/pallas_call | solution.py:485

commit v4 on v3

--- a/solution.py
+++ b/solution.py
@@ -333,35 +333,37 @@
         slope(q)
         ship_slope(q)
 
-    loads[2].wait()
-    turn_acts(4)
     loads[0].wait()
     loads[1].wait()
     slope(0)
     pl.semaphore_wait(barrier, len(partners))
     send_slope(0)
+    loads[2].wait()
+    turn_acts(4)
     ship_acts()
     ship_slope(0)
     send_acts(5)
+    send_acts(3)
     loads[3].wait()
     loads[4].wait()
     own_slice(1)
     send_slope(1)
-    send_acts(3)
-    for cp in [loads[5]] + w_loads:
-        cp.start()
+
+    def load_weight(_):
+        for cp in [loads[5]] + w_loads:
+            cp.start()
 
     plan = (
-        ("S3 S2 G2 G3", "F0 S4 H5 G4", "W0 A6 F1 H3", "S5 G5 100 F2", "A2 U6 H6 W2",)
-        + ("U7 102 F3 W1", "001 U8 A7 W3", "003 H2 U9 U10", "U11 110 A1 F4", "112 H7 T8 013",)
-        + ("011 W4 104 T9", "H1 F5 A0 122", "120 W5 005 I4", "F7 H9 F6 114", "023 021 H8 W6",)
-        + ("F8 I0 H0 015", "F9 J4 W8 I2", "012 010 W9 113", "J0 124 F10 I5", "D4 J2 W10 014",)
-        + ("025 D0 F11 123", "022 J5 I1 020", "D2 W11 115 133", "D5 I3 024 J1", "I6 J3 W7 111",)
-        + ("125 I7 D1 J6", "032 121 D3 J7", "030 D6 D7 135", "034 131",)
+        ("S2 S5 F0 G2", "S4 H5 W0 A2", "S3 H3 F1 G3", "G4 G5 U6 A6", "F2 100 W1 H2",)
+        + ("L0 001 A1 W2", "102 F3 H6 U7", "U8 U9 W3 003", "A7 U10 011 H1", "F4 U11 112 110",)
+        + ("T8 013 H7 W4", "104 T9 021 F5", "A0 H8 023 122", "120 F6 W5 005", "I6 W6 F7 H9",)
+        + ("I3 W7 010 114", "F8 H0 I1 F9", "W8 015 I5 W9", "113 012 F10 111", "J1 124 J5 W10",)
+        + ("014 025 J3 F11", "I0 022 W11 115", "121 D5 D1 J6", "020 D3 024 J0", "I7 123 I2 D6",)
+        + ("125 I4 032 D0", "J2 131 J7 030", "133 J4 D2 D7", "034 135 D4",)
     )
     does = dict(
         F=forward_slope, A=send_acts, W=wait_slope, H=pass_on, S=own_slice,
-        G=send_slope, T=take_acts, U=spread, I=inputs, J=inputs_on, D=inputs_done,
+        G=send_slope, L=load_weight, T=take_acts, U=spread, I=inputs, J=inputs_on, D=inputs_done,
     )
     for word in " ".join(plan).split():
         if word[0] == "I" and not scaled:

time: 97.3 us -> 95.8 us (0.985)
  Pallas kernels: 96.3 us -> 94.9 us
    pallas_call x1, Pallas kernels: 93.9 us -> 92.4 us  [local(): pl.pallas_call(kernel, out_shape=shapes, in_specs=[hbm] * 5, out_specs=(h...]
where the time goes in v4:
time: 95.8 us; the launch traced here: 95.7 us
  Pallas kernels  94.9 us (99%)
    pallas_call x1, Pallas kernels, local(): pl.pallas_call(kernel, out_shape=shapes, in_specs=[hbm] * 5, out_specs=(h...  92.4 us
    pallas_call x1, Pallas kernels, local(): pl.pallas_call(copy_out, out_shape=shapes, in_specs=[hbm] * 2, out_specs=...  2.44 us

profile of v4, /device:TPU:1, one launch (start us, length us, event | category | flops | bytes accessed | tf_op | source)
XLA Modules:
  0.0 95.7 jit_solution(6467848622897293562)
XLA Ops:
  0.6 92.4 %shard_map.68 = (bf16[128,3712]{1,0:T(8,128)(2,1)}, bf16[232,2048]{1,0:T(8,128)(2,1)}) custom-call(bf16[128,3712]{1,0:T(8,128)(2,1)} %acts_h.1, bf16[128,2048]{1,0:T(8,128)(2,1)} %pre_h.1, bf16[128,2048]{1,0:T(8,128)(2,1)} %grad_h.1, bf16[3712,2048]{1,0:T(8,128)(2,1)} %qw_h.1, f32[29,2048]{1,0:T(8,128)} %scale_h.1), custom_call_target="tpu_custom_call" | custom-call | flops 15569256448 | bytes 20971520 | tf_op jit(solution)/shard_map/pallas_call | solution.py:444
  93.1 2.4 %shard_map.69 = (bf16[128,3712]{1,0:T(8,128)(2,1)}, bf16[232,2048]{1,0:T(8,128)(2,1)}) custom-call(bf16[128,3712]{1,0:T(8,128)(2,1)} %get-tuple-element.4.gi_in, bf16[232,2048]{1,0:T(8,128)(2,1)} %get-tuple-element.5.gw_in), custom_call_target="tpu_custom_call" | custom-call | tf_op jit(solution)/shard_map/pallas_call | solution.py:487

commit v5 on v4

--- a/solution.py
+++ b/solution.py
@@ -382,12 +382,6 @@
     for i in range(NP + 1):
         if i not in summed:
             inputs_done(i)
-    wait(go.at[:, pl.ds(0, MID)], s_recv)
-    out_i = pltpu.make_async_copy(go, gi_h, out_sem.at[0])
-    out_i.start()
-    for q in range(NS):
-        add_long(q)
-
     for q in range(NS):
         wait(gb.at[pl.ds(0, 3 * TOK), hidden(q)], g_send.at[q])
         wait(gb.at[pl.ds(0, NY * TOK), hidden(q)], f_send.at[q])
@@ -404,13 +398,22 @@
             wait(at.at[d, :, pl.ds(0, 2 * TOK)], h_send.at[d])
     for way in (0, 1):
         for q in range(NS):
-            for r in range(1, 4) if is_long(way, q) else range(3):
+            for r in range(1, 3) if is_long(way, q) else range(3):
                 wait(landing(way, r, q), z_send.at[way, r, q])
     for i in range(NP):
         wait(gia.at[i], j_send.at[i])
         wait(gir.at[i], i_send.at[i])
     wait(giam, j_send.at[NP])
     wait(girm, i_send.at[NP])
+    wait(go.at[:, pl.ds(0, MID)], s_recv)
+    out_i = pltpu.make_async_copy(go, gi_h, out_sem.at[0])
+    out_i.start()
+    for q in range(NS):
+        add_long(q)
+
+    for q in range(NS):
+        way = 0 if is_long(0, q) else 1
+        wait(landing(way, 3, q), z_send.at[way, 3, q])
     wait(go.at[:, pl.ds(0, MID)], s_send)
     out_i.wait()
     for q in range(NS):

time: 95.8 us -> 95.8 us (level)
  no operation moved by 1% of the time
where the time goes in v5:
time: 95.8 us; the launch traced here: 95.7 us
  Pallas kernels  94.9 us (99%)
    pallas_call x1, Pallas kernels, local(): pl.pallas_call(kernel, out_shape=shapes, in_specs=[hbm] * 5, out_specs=(h...  92.4 us
    pallas_call x1, Pallas kernels, local(): pl.pallas_call(copy_out, out_shape=shapes, in_specs=[hbm] * 2, out_specs=...  2.44 us

profile of v5, /device:TPU:1, one launch (start us, length us, event | category | flops | bytes accessed | tf_op | source)
XLA Modules:
  0.0 95.7 jit_solution(10015727500204293993)
XLA Ops:
  0.6 92.4 %shard_map.68 = (bf16[128,3712]{1,0:T(8,128)(2,1)}, bf16[232,2048]{1,0:T(8,128)(2,1)}) custom-call(bf16[128,3712]{1,0:T(8,128)(2,1)} %acts_h.1, bf16[128,2048]{1,0:T(8,128)(2,1)} %pre_h.1, bf16[128,2048]{1,0:T(8,128)(2,1)} %grad_h.1, bf16[3712,2048]{1,0:T(8,128)(2,1)} %qw_h.1, f32[29,2048]{1,0:T(8,128)} %scale_h.1), custom_call_target="tpu_custom_call" | custom-call | flops 15569256448 | bytes 20971520 | tf_op jit(solution)/shard_map/pallas_call | solution.py:447
  93.1 2.4 %shard_map.69 = (bf16[128,3712]{1,0:T(8,128)(2,1)}, bf16[232,2048]{1,0:T(8,128)(2,1)}) custom-call(bf16[128,3712]{1,0:T(8,128)(2,1)} %get-tuple-element.4.gi_in, bf16[232,2048]{1,0:T(8,128)(2,1)} %get-tuple-element.5.gw_in), custom_call_target="tpu_custom_call" | custom-call | tf_op jit(solution)/shard_map/pallas_call | solution.py:490
